TPU v7x, 32 devices: a whole 2x2x4 slice. The times are simulated.
32 devices in a mesh: image: 8 (over z, x), domain: 4 (over y, core).
Axes of the slice: x: 2, y: 2, z: 4, core: 2. Of those that a mesh axis runs over, the one named last changes fastest.
Arguments:
- field: float32 [8, 16, 64, 128], P('image', 'domain'), may hold values from -0.9 to 1.1
- mobility: float32 [16, 64, 128], P('domain'), may hold values from 0.2 to 1
- lower: int32 [2, 8], P(None, 'image'), may hold values from 0 to 6, as said below
- weights: float32 [2, 8], P(None, 'image'), may hold values from 0 to 1
Outputs:
- evolved: float32 [8, 16, 64, 128], P('image', 'domain')
- arclength: float32 [2, 8], P(None, 'image')
Inputs may be any that keep to these rules, and one draw needn't show every extreme that they name: lower[c, i] is i - 1 or i.
All inputs are finite; a program needn't handle non-finite values.
Results may differ from a plain program's by a relative error of at most 0.0001.
Values sent between devices are 32-bit elements; how exact they have to be, the bound alone decides.
A program may use at most 64 MiB of HBM per device.

v0:
```python
import jax
import jax.numpy as jnp
from jax import lax
from jax.sharding import PartitionSpec as P

STEPS = 8
CYCLES = 2


stiffness = 1.0
time_step = 0.008
epsilon = 1e-06


def extended(shard, sides, width):
    for axis, dim in sides:
        size, length = (lax.axis_size(axis), shard.shape[dim])
        up = [(i, (i + 1) % size) for i in range(size)]
        down = [(j, i) for i, j in up]
        last = lax.slice_in_dim(shard, length - width, length, axis=dim)
        initial = lax.slice_in_dim(shard, 0, width, axis=dim)
        before = lax.ppermute(last, axis, up)
        after = lax.ppermute(initial, axis, down)
        shard = jnp.concatenate([before, shard, after], axis=dim)
    return shard


def passed_along(value, axis, steps):
    count = lax.axis_size(axis)
    initial, last = (max(0, -steps), min(count, count - steps))
    return lax.ppermute(value, axis, [(source, source + steps) for source in range(initial, last)])


def carried_in(value, axis, join, neutral):
    count, mine = (lax.axis_size(axis), lax.axis_index(axis))
    pieces = lax.all_gather(value, axis)
    running = jnp.full_like(value, 0) + jnp.asarray(neutral, value.dtype)

    def lap(position, running):
        longer = join(running, pieces[position])
        return jnp.where(position < mine, longer, running)

    return lax.fori_loop(0, count - 1, lap, running)


def advance(padded, mobile_padded):
    interior = padded[1:-1]
    laplacian = (
        padded[2:]
        + padded[:-2]
        + jnp.roll(interior, 1, 1)
        + jnp.roll(interior, -1, 1)
        + jnp.roll(interior, 1, 2)
        + jnp.roll(interior, -1, 2)
        - 6.0 * interior
    )
    potential = interior * interior * interior - interior - stiffness * laplacian
    motion = mobile_padded[1:-1] / (1.0 + interior * interior)
    centre = motion[1:-1]
    middle = potential[1:-1]
    change = 0.5 * (centre + motion[2:]) * (potential[2:] - middle) + 0.5 * (
        centre + motion[:-2]
    ) * (potential[:-2] - middle)
    for dimension in (1, 2):
        for offset in (1, -1):
            change = change + 0.5 * (centre + jnp.roll(centre, offset, dimension)) * (
                jnp.roll(middle, offset, dimension) - middle
            )
    return padded[2:-2] + time_step * change


def add_terms(earlier, later):
    return earlier + later


def per_device(field, mobility, lower, weights):
    domain_count = lax.axis_size("domain")
    image_count = lax.axis_size("image")
    image_index = lax.axis_index("image")
    phase_field = field[0]
    total_cells = phase_field.shape[0] * domain_count * phase_field.shape[1] * phase_field.shape[2]
    per_exchange = 2
    rim_depth = 2 * per_exchange
    mobile_wide = extended(mobility, (("domain", 0),), rim_depth)
    lengths = []
    for cycle_index in range(CYCLES):
        for step_start in range(0, STEPS, per_exchange):
            padded = extended(phase_field, (("domain", 0),), 4)
            for repeat in range(per_exchange):
                margin = 2 * repeat
                padded = advance(padded, mobile_wide[margin : mobile_wide.shape[0] - margin])
            phase_field = padded
        left_field = passed_along(phase_field, "image", 1)
        right_field = passed_along(phase_field, "image", -1)
        local_sum = jnp.sum(jnp.square(right_field - phase_field))
        gap_total = lax.psum(local_sum, "domain")
        distance = jnp.sqrt(gap_total / total_cells + epsilon)
        distance = jnp.where(image_index == image_count - 1, jnp.float32(0.0), distance)
        arclength = carried_in(distance, "image", add_terms, jnp.float32(0.0))
        lengths.append(arclength)
        weight_now = weights[cycle_index, 0]
        lower_now = lower[cycle_index, 0]
        from_left = lower_now < image_index
        first_image = jnp.where(from_left, left_field, phase_field)
        second_image = jnp.where(from_left, phase_field, right_field)
        phase_field = weight_now * first_image + (1.0 - weight_now) * second_image
    return (phase_field[None], jnp.stack(lengths)[:, None])


def solution(mesh):
    return jax.shard_map(
        per_device,
        mesh=mesh,
        in_specs=(
            P("image", "domain", None, None),
            P("domain", None, None),
            P(None, "image"),
            P(None, "image"),
        ),
        out_specs=(P("image", "domain", None, None), P(None, "image")),
        check_vma=False,
    )
```

profile of v0, /device:TPU:0, one launch (start us, length us, event | category | flops | bytes accessed | tf_op | source)
XLA Modules:
  0.0 145.5 jit_solution(9268191320415341360)
XLA Ops:
  1.1 2.0 %collective-permute-start.1 = (f32[4,64,128]{2,1,0:T(8,128)}, f32[4,64,128]{2,1,0:T(8,128)S(1)}, u32[]{:S(2)}, u32[]{:S(2)}) collective-permute-start(f32[4,64,128]{2,1,0:T(8,128)} %bitcast.21), channel_id=1, source_target_pairs={{1,0},{2,1},{3,2},{0,3},{5,4},{6,5},{7,6},{4,7},{9,8},{10,9},{11,1... | collective-permute-start | bytes 393224 | tf_op jit(solution)/shard_map/ppermute | solution.py:23
  3.8 1.1 collective-permute-start.3
  4.9 1.1 collective-permute-done
  6.0 1.4 collective-permute-done.1
  13.2 1.7 %collective-permute-start.4 = (f32[4,64,128]{2,1,0:T(8,128)S(1)}, f32[4,64,128]{2,1,0:T(8,128)S(1)}, u32[]{:S(2)}, u32[]{:S(2)}) collective-permute-start(f32[4,64,128]{2,1,0:T(8,128)S(1)} %fusion.364), channel_id=1, source_target_pairs={{0,1},{1,2},{2,3},{3,0},{4,5},{5,6},{6,7},{7,4},{8,9},{9,10},{10,1... | collective-permute-start | bytes 393224 | tf_op jit(solution)/shard_map/ppermute | solution.py:22
  15.4 2.6 %collective-permute-done.4 = f32[4,64,128]{2,1,0:T(8,128)S(1)} collective-permute-done((f32[4,64,128]{2,1,0:T(8,128)S(1)}, f32[4,64,128]{2,1,0:T(8,128)S(1)}, u32[]{:S(2)}, u32[]{:S(2)}) %collective-permute-start.4) | collective-permute-done | bytes 131104 | tf_op jit(solution)/shard_map/ppermute | solution.py:22
  18.0 1.2 collective-permute-done.5
  22.4 1.4 collective-permute-start.6
  24.7 2.6 %collective-permute-done.6 = f32[4,64,128]{2,1,0:T(8,128)S(1)} collective-permute-done((f32[4,64,128]{2,1,0:T(8,128)S(1)}, f32[4,64,128]{2,1,0:T(8,128)S(1)}, u32[]{:S(2)}, u32[]{:S(2)}) %collective-permute-start.6) | collective-permute-done | bytes 131104 | tf_op jit(solution)/shard_map/ppermute | solution.py:22
  27.3 1.0 collective-permute-done.7
  31.5 1.2 collective-permute-start.8
  33.6 2.6 %collective-permute-done.8 = f32[4,64,128]{2,1,0:T(8,128)S(1)} collective-permute-done((f32[4,64,128]{2,1,0:T(8,128)S(1)}, f32[4,64,128]{2,1,0:T(8,128)S(1)}, u32[]{:S(2)}, u32[]{:S(2)}) %collective-permute-start.8) | collective-permute-done | bytes 131104 | tf_op jit(solution)/shard_map/ppermute | solution.py:22
  40.3 1.4 collective-permute-start.10
  41.7 1.3 collective-permute-start.11
  45.6 4.2 %collective-permute-done.11 = f32[4,64,128]{2,1,0:T(8,128)S(1)} collective-permute-done((f32[4,64,128]{2,1,0:T(8,128)S(1)}, f32[4,64,128]{2,1,0:T(8,128)S(1)}, u32[]{:S(2)}, u32[]{:S(2)}) %collective-permute-start.11) | collective-permute-done | bytes 131104 | tf_op jit(solution)/shard_map/ppermute | solution.py:31
  49.9 1.4 multiply_reduce_fusion.1
  51.3 1.6 %collective-permute-start.13 = (f32[4,64,128]{2,1,0:T(8,128)S(1)}, f32[4,64,128]{2,1,0:T(8,128)S(1)}, u32[]{:S(2)}, u32[]{:S(2)}) collective-permute-start(f32[4,64,128]{2,1,0:T(8,128)S(1)} %get-tuple-element.375), channel_id=1, source_target_pairs={{1,0},{2,1},{3,2},{0,3},{5,4},{6,5},{7,6},{4,7},{9,8},{10,9},{11,1... | collective-permute-start | bytes 393224 | tf_op jit(solution)/shard_map/ppermute | solution.py:23
  53.0 2.6 %collective-permute-done.12 = f32[4,64,128]{2,1,0:T(8,128)S(1)} collective-permute-done((f32[4,64,128]{2,1,0:T(8,128)S(1)}, f32[4,64,128]{2,1,0:T(8,128)S(1)}, u32[]{:S(2)}, u32[]{:S(2)}) %collective-permute-start.12) | collective-permute-done | bytes 131104 | tf_op jit(solution)/shard_map/ppermute | solution.py:22
  59.2 1.2 collective-permute-start.14
  61.2 2.6 %collective-permute-done.14 = f32[4,64,128]{2,1,0:T(8,128)S(1)} collective-permute-done((f32[4,64,128]{2,1,0:T(8,128)S(1)}, f32[4,64,128]{2,1,0:T(8,128)S(1)}, u32[]{:S(2)}, u32[]{:S(2)}) %collective-permute-start.14) | collective-permute-done | bytes 131104 | tf_op jit(solution)/shard_map/ppermute | solution.py:22
  67.4 1.2 collective-permute-start.16
  69.4 2.6 %collective-permute-done.16 = f32[4,64,128]{2,1,0:T(8,128)S(1)} collective-permute-done((f32[4,64,128]{2,1,0:T(8,128)S(1)}, f32[4,64,128]{2,1,0:T(8,128)S(1)}, u32[]{:S(2)}, u32[]{:S(2)}) %collective-permute-start.16) | collective-permute-done | bytes 131104 | tf_op jit(solution)/shard_map/ppermute | solution.py:22
  75.5 1.2 collective-permute-start.18
  77.5 2.6 %collective-permute-done.18 = f32[4,64,128]{2,1,0:T(8,128)S(1)} collective-permute-done((f32[4,64,128]{2,1,0:T(8,128)S(1)}, f32[4,64,128]{2,1,0:T(8,128)S(1)}, u32[]{:S(2)}, u32[]{:S(2)}) %collective-permute-start.18) | collective-permute-done | bytes 131104 | tf_op jit(solution)/shard_map/ppermute | solution.py:22
  83.5 3.1 %collective-permute-start.20 = (f32[4,64,128]{2,1,0:T(8,128)S(1)}, f32[4,64,128]{2,1,0:T(8,128)S(1)}, u32[]{:S(2)}, u32[]{:S(2)}) collective-permute-start(f32[4,64,128]{2,1,0:T(8,128)S(1)} %fusion.287), channel_id=1, source_target_pairs={{0,4},{4,8},{8,12},{12,16},{16,20},{20,24},{24,28},{1,5},{5,9},{9,... | collective-permute-start | bytes 393224 | tf_op jit(solution)/shard_map/ppermute | solution.py:31
  86.7 1.3 collective-permute-start.21
  90.6 4.3 %collective-permute-done.21 = f32[4,64,128]{2,1,0:T(8,128)S(1)} collective-permute-done((f32[4,64,128]{2,1,0:T(8,128)S(1)}, f32[4,64,128]{2,1,0:T(8,128)S(1)}, u32[]{:S(2)}, u32[]{:S(2)}) %collective-permute-start.21) | collective-permute-done | bytes 131104 | tf_op jit(solution)/shard_map/ppermute | solution.py:31
  94.9 1.9 %multiply_reduce_fusion = (f32[]{:T(128)}, f32[1,4,64,128]{3,2,1,0:T(8,128)}) fusion(f32[4,64,128]{2,1,0:T(8,128)S(1)} %collective-permute-done.21, f32[4,64,128]{2,1,0:T(8,128)S(1)} %fusion.287, f32[]{:T(128)S(6)} %sub.589, f32[4,64,128]{2,1,0:T(8,128)S(1)} %collective-permute-done.20, pred[]{:T(512)S(6)} %lt.40, f32[]{:T(128)} %bitcast.2), kind=kLoop, calls=%fused_computation.712 | loop fusion | flops 262143 | bytes 524301 | tf_op jit(solution)/shard_map/reduce_sum | solution.py:95
  96.9 7.1 %all-reduce.3 = (f32[]{:T(128)}, f32[]{:T(128)}) all-reduce(f32[]{:T(128)} %get-tuple-element.376, f32[]{:T(128)} %get-tuple-element.374), channel_id=1, replica_groups=mesh['image'=8,'domain'=4] {'domain'}, use_global_device_ids=true, to_apply=%region_5.6 | all-reduce | flops 2 | bytes 16 | tf_op jit(solution)/shard_map/psum | solution.py:96
  106.8 20.5 %all-reduce.2 = (f32[8]{0:T(128)S(1)}, f32[8]{0:T(128)S(1)}) all-reduce(f32[8]{0:T(128)S(1)} %dynamic-update-slice.1, f32[8]{0:T(128)S(1)} %dynamic-update-slice), channel_id=1, replica_groups=mesh['image'=8,'domain'=4] {'image'}, use_global_device_ids=true, to_apply=%add.1 | all-reduce | flops 16 | bytes 128
  127.3 8.8 %while.26 = (s32[]{:T(128)}, f32[]{:T(128)}, s32[]{:T(128)}, f32[8]{0:T(128)S(1)}, s32[]{:T(128)}) while((s32[]{:T(128)}, f32[]{:T(128)}, s32[]{:T(128)}, f32[8]{0:T(128)S(1)}, s32[]{:T(128)}) %tuple.270), condition=%wide.region_3.4_spmd, body=%wide.region_2.3_spmd.sunk | while | flops 5 | bytes 107 | solution.py:43
  136.1 8.8 %while.27 = (s32[]{:T(128)}, f32[]{:T(128)}, s32[]{:T(128)}, f32[8]{0:T(128)S(1)}, s32[]{:T(128)}) while((s32[]{:T(128)}, f32[]{:T(128)}, s32[]{:T(128)}, f32[8]{0:T(128)S(1)}, s32[]{:T(128)}) %tuple.267), condition=%wide.region_7.8_spmd, body=%wide.region_6.7_spmd.sunk | while | flops 5 | bytes 107 | solution.py:43
  (273 shorter events, 47.7 us)
Async XLA Ops:
  0.6 5.3 %collective-permute-start = (f32[4,64,128]{2,1,0:T(8,128)}, f32[4,64,128]{2,1,0:T(8,128)S(1)}, u32[]{:S(2)}, u32[]{:S(2)}) collective-permute-start(f32[4,64,128]{2,1,0:T(8,128)} %bitcast.20), channel_id=1, source_target_pairs={{0,1},{1,2},{2,3},{3,0},{4,5},{5,6},{6,7},{7,4},{8,9},{9,10},{10,1... | collective-permute-start | bytes 393224 | tf_op jit(solution)/shard_map/ppermute | solution.py:22
  1.1 6.2 %collective-permute-start.1 = (f32[4,64,128]{2,1,0:T(8,128)}, f32[4,64,128]{2,1,0:T(8,128)S(1)}, u32[]{:S(2)}, u32[]{:S(2)}) collective-permute-start(f32[4,64,128]{2,1,0:T(8,128)} %bitcast.21), channel_id=1, source_target_pairs={{1,0},{2,1},{3,2},{0,3},{5,4},{6,5},{7,6},{4,7},{9,8},{10,9},{11,1... | collective-permute-start | bytes 393224 | tf_op jit(solution)/shard_map/ppermute | solution.py:23
  3.2 5.5 %collective-permute-start.2 = (f32[4,64,128]{2,1,0:T(8,128)}, f32[4,64,128]{2,1,0:T(8,128)S(1)}, u32[]{:S(2)}, u32[]{:S(2)}) collective-permute-start(f32[4,64,128]{2,1,0:T(8,128)} %param.9), channel_id=1, source_target_pairs={{0,1},{1,2},{2,3},{3,0},{4,5},{5,6},{6,7},{7,4},{8,9},{9,10},{10,1... | collective-permute-start | bytes 393224 | tf_op jit(solution)/shard_map/ppermute | solution.py:22
  3.8 6.3 %collective-permute-start.3 = (f32[4,64,128]{2,1,0:T(8,128)}, f32[4,64,128]{2,1,0:T(8,128)S(1)}, u32[]{:S(2)}, u32[]{:S(2)}) collective-permute-start(f32[4,64,128]{2,1,0:T(8,128)} %param.9), channel_id=1, source_target_pairs={{1,0},{2,1},{3,2},{0,3},{5,4},{6,5},{7,6},{4,7},{9,8},{10,9},{11,1... | collective-permute-start | bytes 393224 | tf_op jit(solution)/shard_map/ppermute | solution.py:23
  8.7 0.9 copy-start.1
  9.6 0.9 copy-start
  13.2 4.8 %collective-permute-start.4 = (f32[4,64,128]{2,1,0:T(8,128)S(1)}, f32[4,64,128]{2,1,0:T(8,128)S(1)}, u32[]{:S(2)}, u32[]{:S(2)}) collective-permute-start(f32[4,64,128]{2,1,0:T(8,128)S(1)} %fusion.364), channel_id=1, source_target_pairs={{0,1},{1,2},{2,3},{3,0},{4,5},{5,6},{6,7},{7,4},{8,9},{9,10},{10,1... | collective-permute-start | bytes 393224 | tf_op jit(solution)/shard_map/ppermute | solution.py:22
  14.8 4.3 %collective-permute-start.5 = (f32[4,64,128]{2,1,0:T(8,128)S(1)}, f32[4,64,128]{2,1,0:T(8,128)S(1)}, u32[]{:S(2)}, u32[]{:S(2)}) collective-permute-start(f32[4,64,128]{2,1,0:T(8,128)S(1)} %fusion.364), channel_id=1, source_target_pairs={{1,0},{2,1},{3,2},{0,3},{5,4},{6,5},{7,6},{4,7},{9,8},{10,9},{11,1... | collective-permute-start | bytes 393224 | tf_op jit(solution)/shard_map/ppermute | solution.py:23
  22.4 4.9 %collective-permute-start.6 = (f32[4,64,128]{2,1,0:T(8,128)S(1)}, f32[4,64,128]{2,1,0:T(8,128)S(1)}, u32[]{:S(2)}, u32[]{:S(2)}) collective-permute-start(f32[4,64,128]{2,1,0:T(8,128)S(1)} %fusion.353), channel_id=1, source_target_pairs={{0,1},{1,2},{2,3},{3,0},{4,5},{5,6},{6,7},{7,4},{8,9},{9,10},{10,1... | collective-permute-start | bytes 393224 | tf_op jit(solution)/shard_map/ppermute | solution.py:22
  23.8 4.5 %collective-permute-start.7 = (f32[4,64,128]{2,1,0:T(8,128)S(1)}, f32[4,64,128]{2,1,0:T(8,128)S(1)}, u32[]{:S(2)}, u32[]{:S(2)}) collective-permute-start(f32[4,64,128]{2,1,0:T(8,128)S(1)} %fusion.353), channel_id=1, source_target_pairs={{1,0},{2,1},{3,2},{0,3},{5,4},{6,5},{7,6},{4,7},{9,8},{10,9},{11,1... | collective-permute-start | bytes 393224 | tf_op jit(solution)/shard_map/ppermute | solution.py:23
  31.5 4.6 %collective-permute-start.8 = (f32[4,64,128]{2,1,0:T(8,128)S(1)}, f32[4,64,128]{2,1,0:T(8,128)S(1)}, u32[]{:S(2)}, u32[]{:S(2)}) collective-permute-start(f32[4,64,128]{2,1,0:T(8,128)S(1)} %fusion.342), channel_id=1, source_target_pairs={{0,1},{1,2},{2,3},{3,0},{4,5},{5,6},{6,7},{7,4},{8,9},{9,10},{10,1... | collective-permute-start | bytes 393224 | tf_op jit(solution)/shard_map/ppermute | solution.py:22
  32.8 4.3 %collective-permute-start.9 = (f32[4,64,128]{2,1,0:T(8,128)S(1)}, f32[4,64,128]{2,1,0:T(8,128)S(1)}, u32[]{:S(2)}, u32[]{:S(2)}) collective-permute-start(f32[4,64,128]{2,1,0:T(8,128)S(1)} %fusion.342), channel_id=1, source_target_pairs={{1,0},{2,1},{3,2},{0,3},{5,4},{6,5},{7,6},{4,7},{9,8},{10,9},{11,1... | collective-permute-start | bytes 393224 | tf_op jit(solution)/shard_map/ppermute | solution.py:23
  40.1 3.0 %copy-start.2 = (s32[2,1]{0,1:T(1,128)S(1)}, s32[2,1]{0,1:T(1,128)}, u32[]{:S(2)}) copy-start(s32[2,1]{0,1:T(1,128)} %param.10) | copy-start | bytes 28
  40.3 5.3 %collective-permute-start.10 = (f32[4,64,128]{2,1,0:T(8,128)S(1)}, f32[4,64,128]{2,1,0:T(8,128)S(1)}, u32[]{:S(2)}, u32[]{:S(2)}) collective-permute-start(f32[4,64,128]{2,1,0:T(8,128)S(1)} %fusion.331), channel_id=1, source_target_pairs={{0,4},{4,8},{8,12},{12,16},{16,20},{20,24},{24,28},{1,5},{5,9},{9,... | collective-permute-start | bytes 393224 | tf_op jit(solution)/shard_map/ppermute | solution.py:31
  41.7 8.1 %collective-permute-start.11 = (f32[4,64,128]{2,1,0:T(8,128)S(1)}, f32[4,64,128]{2,1,0:T(8,128)S(1)}, u32[]{:S(2)}, u32[]{:S(2)}) collective-permute-start(f32[4,64,128]{2,1,0:T(8,128)S(1)} %fusion.331), channel_id=1, source_target_pairs={{4,0},{8,4},{12,8},{16,12},{20,16},{24,20},{28,24},{5,1},{9,5},{13... | collective-permute-start | bytes 393224 | tf_op jit(solution)/shard_map/ppermute | solution.py:31
  43.7 0.7 copy-start.3
  51.2 4.4 %collective-permute-start.12 = (f32[4,64,128]{2,1,0:T(8,128)S(1)}, f32[4,64,128]{2,1,0:T(8,128)S(1)}, u32[]{:S(2)}, u32[]{:S(2)}) collective-permute-start(f32[4,64,128]{2,1,0:T(8,128)S(1)} %get-tuple-element.375), channel_id=1, source_target_pairs={{0,1},{1,2},{2,3},{3,0},{4,5},{5,6},{6,7},{7,4},{8,9},{9,10},{10,1... | collective-permute-start | bytes 393224 | tf_op jit(solution)/shard_map/ppermute | solution.py:22
  51.3 4.6 %collective-permute-start.13 = (f32[4,64,128]{2,1,0:T(8,128)S(1)}, f32[4,64,128]{2,1,0:T(8,128)S(1)}, u32[]{:S(2)}, u32[]{:S(2)}) collective-permute-start(f32[4,64,128]{2,1,0:T(8,128)S(1)} %get-tuple-element.375), channel_id=1, source_target_pairs={{1,0},{2,1},{3,2},{0,3},{5,4},{6,5},{7,6},{4,7},{9,8},{10,9},{11,1... | collective-permute-start | bytes 393224 | tf_op jit(solution)/shard_map/ppermute | solution.py:23
  59.2 4.6 %collective-permute-start.14 = (f32[4,64,128]{2,1,0:T(8,128)S(1)}, f32[4,64,128]{2,1,0:T(8,128)S(1)}, u32[]{:S(2)}, u32[]{:S(2)}) collective-permute-start(f32[4,64,128]{2,1,0:T(8,128)S(1)} %fusion.320), channel_id=1, source_target_pairs={{0,1},{1,2},{2,3},{3,0},{4,5},{5,6},{6,7},{7,4},{8,9},{9,10},{10,1... | collective-permute-start | bytes 393224 | tf_op jit(solution)/shard_map/ppermute | solution.py:22
  60.4 3.7 %collective-permute-start.15 = (f32[4,64,128]{2,1,0:T(8,128)S(1)}, f32[4,64,128]{2,1,0:T(8,128)S(1)}, u32[]{:S(2)}, u32[]{:S(2)}) collective-permute-start(f32[4,64,128]{2,1,0:T(8,128)S(1)} %fusion.320), channel_id=1, source_target_pairs={{1,0},{2,1},{3,2},{0,3},{5,4},{6,5},{7,6},{4,7},{9,8},{10,9},{11,1... | collective-permute-start | bytes 393224 | tf_op jit(solution)/shard_map/ppermute | solution.py:23
  67.4 4.6 %collective-permute-start.16 = (f32[4,64,128]{2,1,0:T(8,128)S(1)}, f32[4,64,128]{2,1,0:T(8,128)S(1)}, u32[]{:S(2)}, u32[]{:S(2)}) collective-permute-start(f32[4,64,128]{2,1,0:T(8,128)S(1)} %fusion.309), channel_id=1, source_target_pairs={{0,1},{1,2},{2,3},{3,0},{4,5},{5,6},{6,7},{7,4},{8,9},{9,10},{10,1... | collective-permute-start | bytes 393224 | tf_op jit(solution)/shard_map/ppermute | solution.py:22
  68.6 3.7 %collective-permute-start.17 = (f32[4,64,128]{2,1,0:T(8,128)S(1)}, f32[4,64,128]{2,1,0:T(8,128)S(1)}, u32[]{:S(2)}, u32[]{:S(2)}) collective-permute-start(f32[4,64,128]{2,1,0:T(8,128)S(1)} %fusion.309), channel_id=1, source_target_pairs={{1,0},{2,1},{3,2},{0,3},{5,4},{6,5},{7,6},{4,7},{9,8},{10,9},{11,1... | collective-permute-start | bytes 393224 | tf_op jit(solution)/shard_map/ppermute | solution.py:23
  75.5 4.6 %collective-permute-start.18 = (f32[4,64,128]{2,1,0:T(8,128)S(1)}, f32[4,64,128]{2,1,0:T(8,128)S(1)}, u32[]{:S(2)}, u32[]{:S(2)}) collective-permute-start(f32[4,64,128]{2,1,0:T(8,128)S(1)} %fusion.298), channel_id=1, source_target_pairs={{0,1},{1,2},{2,3},{3,0},{4,5},{5,6},{6,7},{7,4},{8,9},{9,10},{10,1... | collective-permute-start | bytes 393224 | tf_op jit(solution)/shard_map/ppermute | solution.py:22
  76.7 3.6 %collective-permute-start.19 = (f32[4,64,128]{2,1,0:T(8,128)S(1)}, f32[4,64,128]{2,1,0:T(8,128)S(1)}, u32[]{:S(2)}, u32[]{:S(2)}) collective-permute-start(f32[4,64,128]{2,1,0:T(8,128)S(1)} %fusion.298), channel_id=1, source_target_pairs={{1,0},{2,1},{3,2},{0,3},{5,4},{6,5},{7,6},{4,7},{9,8},{10,9},{11,1... | collective-permute-start | bytes 393224 | tf_op jit(solution)/shard_map/ppermute | solution.py:23
  83.5 7.1 %collective-permute-start.20 = (f32[4,64,128]{2,1,0:T(8,128)S(1)}, f32[4,64,128]{2,1,0:T(8,128)S(1)}, u32[]{:S(2)}, u32[]{:S(2)}) collective-permute-start(f32[4,64,128]{2,1,0:T(8,128)S(1)} %fusion.287), channel_id=1, source_target_pairs={{0,4},{4,8},{8,12},{12,16},{16,20},{20,24},{24,28},{1,5},{5,9},{9,... | collective-permute-start | bytes 393224 | tf_op jit(solution)/shard_map/ppermute | solution.py:31
  86.7 8.2 %collective-permute-start.21 = (f32[4,64,128]{2,1,0:T(8,128)S(1)}, f32[4,64,128]{2,1,0:T(8,128)S(1)}, u32[]{:S(2)}, u32[]{:S(2)}) collective-permute-start(f32[4,64,128]{2,1,0:T(8,128)S(1)} %fusion.287), channel_id=1, source_target_pairs={{4,0},{8,4},{12,8},{16,12},{20,16},{24,20},{28,24},{5,1},{9,5},{13... | collective-permute-start | bytes 393224 | tf_op jit(solution)/shard_map/ppermute | solution.py:31
  89.3 0.7 copy-start.4
where the time goes:
time: 146 us
  waiting for transfers between devices  34.1 us (23%)
  blocking collectives  27.6 us (19%)
  local copies, waits for them, and re-layouts  27 us (18%)
  starting transfers between devices  25.8 us (18%)
  other arithmetic  15.5 us (11%)
  loops' own time  9.38 us (6%)
  between operations  6.15 us (4%)
    unnamed x1, blocking collectives  20.5 us
    ppermute x9, waiting for transfers between devices, extended(): before = lax.ppermute(last, axis, up)  19.2 us
    another operation x2, loops' own time, carried_in(): return lax.fori_loop(0, count - 1, lap, running)  9.38 us
    ppermute x9, starting transfers between devices, extended(): after = lax.ppermute(initial, axis, down)  9.36 us
    ppermute x9, starting transfers between devices, extended(): before = lax.ppermute(last, axis, up)  9.32 us
    ppermute x4, waiting for transfers between devices, passed_along(): lax.ppermute(value, axis, [(source, source + steps) for source in range(i...  8.58 us
    dynamic_slice x14, local copies, waits for them, and re-layouts, lap(): longer = join(running, pieces[position])  8.21 us
    ppermute x4, starting transfers between devices, passed_along(): lax.ppermute(value, axis, [(source, source + steps) for source in range(i...  7.11 us
  transfers between devices with their start and end apart: 22, of which 19 were waited for; matrix products, arithmetic and copies ran while one was open for 2% of the time, Pallas kernels for 0%

commit v1 on v0

v1 whole, which is shorter than its diff:
```python
import functools

import jax
import jax.numpy as jnp
from jax import lax
from jax.experimental import pallas as pl
from jax.experimental.pallas import tpu as pltpu
from jax.sharding import PartitionSpec as P

STEPS = 8
CYCLES = 2
SUBLANES = 8

stiffness = 1.0
time_step = 0.008
epsilon = 1e-06
MESH = pl.DeviceIdType.MESH


def kernel(
    domain_count,
    image_count,
    field_ref,
    mobility_ref,
    lower_ref,
    weights_ref,
    evolved_ref,
    arclength_ref,
    stage,
    ring,
    potential,
    motion,
    partner_field,
    relay_field,
    sums,
    distances,
    stage_sem,
    gather_send,
    gather_recv,
    partner_send,
    partner_recv,
    relay_send,
    relay_recv,
    sum_send,
    sum_recv,
    distance_send,
    distance_recv,
):
    planes, ny, nz = stage.shape[1:]
    rows = ny // SUBLANES
    window = domain_count * planes
    crossings = domain_count // 2 - 1
    image = lax.axis_index("image")
    domain = lax.axis_index("domain")

    field_copy = pltpu.make_async_copy(field_ref.at[0], stage.at[0], stage_sem.at[0])
    mobility_copy = pltpu.make_async_copy(mobility_ref, stage.at[1], stage_sem.at[1])
    field_copy.start()
    mobility_copy.start()

    barrier = pltpu.get_barrier_semaphore()
    for away in range(1, domain_count):
        pl.semaphore_signal(barrier, inc=1, device_id=(image, lax.rem(domain + away, domain_count)), device_id_type=MESH)
    for away in range(1, image_count):
        pl.semaphore_signal(barrier, inc=1, device_id=(lax.rem(image + away, image_count), domain), device_id_type=MESH)

    domain_parity = lax.rem(domain, 2)
    sibling = domain + 1 - 2 * domain_parity
    at_sibling = lax.rem(domain - sibling + domain_count, domain_count)

    def gather_copy(buffer, message, plane):
        if message == 0:
            source, target, slot = 0, sibling, at_sibling
        elif message <= crossings:
            hop = 2 * message
            source, target, slot = 0, lax.rem(domain + hop, domain_count), domain_count - hop
        else:
            hop = 2 * (message - crossings)
            source, target = domain_count - hop, sibling
            slot = lax.rem(at_sibling + domain_count - hop, domain_count)
        return pltpu.make_async_remote_copy(
            src_ref=ring.at[buffer, source * planes + plane],
            dst_ref=ring.at[buffer, slot * planes + plane],
            send_sem=gather_send.at[buffer, message, plane],
            recv_sem=gather_recv.at[buffer, message, plane],
            device_id=(image, target),
            device_id_type=MESH,
        )

    def send_own(buffer, plane):
        for message in range(crossings, -1, -1):
            gather_copy(buffer, message, plane).start()

    def forward(buffer):
        for plane in range(planes):
            for message in range(1, crossings + 1):
                gather_copy(buffer, message, plane).wait_recv()
                gather_copy(buffer, crossings + message, plane).start()

    def finish_gather(buffer):
        for plane in range(planes):
            gather_copy(buffer, 0, plane).wait_recv()
            for message in range(crossings + 1, 2 * crossings + 1):
                gather_copy(buffer, message, plane).wait_recv()

    def drain_gather(buffer):
        for plane in range(planes):
            for message in range(2 * crossings + 1):
                gather_copy(buffer, message, plane).wait_send()

    def load_interleaved(which, buffer):
        for plane in range(planes):
            for row in range(rows):
                ring[buffer, plane, row] = stage[which, plane, pl.ds(row, SUBLANES, stride=rows), :]

    field_copy.wait()
    load_interleaved(0, 0)
    mobility_copy.wait()
    load_interleaved(1, CYCLES)
    pl.semaphore_wait(barrier, domain_count - 1 + image_count - 1)
    for plane in range(planes):
        send_own(0, plane)
    for plane in range(planes):
        send_own(CYCLES, plane)
    forward(0)
    forward(CYCLES)

    def next_row(value):
        return jnp.concatenate([value[1:], pltpu.roll(value[:1], SUBLANES - 1, 1)], axis=0)

    def previous_row(value):
        return jnp.concatenate([pltpu.roll(value[-1:], 1, 1), value[:-1]], axis=0)

    def next_column(value):
        return pltpu.roll(value, nz - 1, 2)

    def previous_column(value):
        return pltpu.roll(value, 1, 2)

    def advance(buffer):
        def step(number, carry):
            reach = 2 * (STEPS - 1 - number)
            offset = (2 * STEPS // window + 1) * window

            def place(index):
                return lax.rem(index, window)

            def potentials(group, carry):
                base = offset - reach - 1 + group * planes
                layers = [ring[buffer, place(base - 1 + k)] for k in range(planes + 2)]
                for k in range(planes):
                    here = layers[k + 1]
                    around = (layers[k] + layers[k + 2]) + (next_row(here) + previous_row(here))
                    around = around + (next_column(here) + previous_column(here))
                    square = here * here
                    potential[place(base + k)] = here * (square + (6.0 * stiffness - 1.0)) - stiffness * around
                    below = 1.0 + square
                    inverse = pl.reciprocal(below, approx=True)
                    inverse = inverse * (2.0 - below * inverse)
                    motion[place(base + k)] = ring[CYCLES, place(base + k)] * inverse
                return carry

            def changes(group, carry):
                base = offset - reach + group * planes
                level = [potential[place(base - 1 + k)] for k in range(planes + 2)]
                speed = [motion[place(base - 1 + k)] for k in range(planes + 2)]
                flux = [(speed[k] + speed[k + 1]) * (level[k + 1] - level[k]) for k in range(planes + 1)]
                for k in range(planes):
                    here, mobile = level[k + 1], speed[k + 1]
                    along_row = (mobile + next_row(mobile)) * (next_row(here) - here)
                    along_column = (mobile + next_column(mobile)) * (next_column(here) - here)
                    change = (flux[k + 1] - flux[k]) + (along_row - previous_row(along_row))
                    change = change + (along_column - previous_column(along_column))
                    ring[buffer, place(base + k)] = ring[buffer, place(base + k)] + (0.5 * time_step) * change
                return carry

            potential_groups = jnp.minimum(domain_count, (2 * planes + 2 * reach + 1) // planes)
            change_groups = jnp.minimum(domain_count, (2 * planes + 2 * reach - 1) // planes)
            lax.fori_loop(0, potential_groups, potentials, 0)
            lax.fori_loop(0, change_groups, changes, 0)
            return carry

        lax.fori_loop(0, STEPS, step, 0)

    image_parity = lax.rem(image, 2)
    odd = image_parity == 1
    partner = image + 1 - 2 * image_parity
    onward = image + 2 - 4 * image_parity
    has_onward = jnp.logical_and(onward >= 0, onward < image_count)
    behind = image - 2 + 4 * image_parity
    has_behind = jnp.logical_and(behind >= 0, behind < image_count)

    def partner_copy(cycle, plane):
        return pltpu.make_async_remote_copy(
            src_ref=ring.at[cycle, plane],
            dst_ref=partner_field.at[cycle, plane],
            send_sem=partner_send.at[cycle, plane],
            recv_sem=partner_recv.at[cycle, plane],
            device_id=(partner, domain),
            device_id_type=MESH,
        )

    def relay_copy(cycle, plane):
        return pltpu.make_async_remote_copy(
            src_ref=partner_field.at[cycle, plane],
            dst_ref=relay_field.at[cycle, plane],
            send_sem=relay_send.at[cycle, plane],
            recv_sem=relay_recv.at[cycle, plane],
            device_id=(onward, domain),
            device_id_type=MESH,
        )

    @pl.when(jnp.logical_not(has_behind))
    def _():
        relay_field[...] = jnp.zeros(relay_field.shape, jnp.float32)

    for cycle in range(CYCLES):
        finish_gather(cycle)
        if cycle == 0:
            finish_gather(CYCLES)
            drain_gather(CYCLES)
        drain_gather(cycle)
        advance(cycle)
        for plane in range(planes):
            partner_copy(cycle, plane).start()
        weight = weights_ref[cycle, 0]
        from_left = lower_ref[cycle, 0] < image
        own_share = jnp.where(from_left, 1.0 - weight, weight)
        other_share = jnp.where(from_left, weight, 1.0 - weight)
        from_left = jnp.where(from_left, 1, 0)
        use_partner = jnp.full((rows, SUBLANES, nz), from_left, jnp.int32) == image_parity
        left_partner = jnp.full((rows, SUBLANES, nz), image_parity, jnp.int32) == 1
        for plane in range(planes):
            partner_copy(cycle, plane).wait_recv()

            @pl.when(has_onward)
            def _():
                relay_copy(cycle, plane).start()

        gap = jnp.zeros((SUBLANES, nz), jnp.float32)
        for plane in range(planes):
            @pl.when(has_behind)
            def _():
                relay_copy(cycle, plane).wait_recv()

            own = ring[cycle, plane]
            by_partner = partner_field[cycle, plane]
            by_relay = relay_field[cycle, plane]
            mixed = own_share * own + other_share * jnp.where(use_partner, by_partner, by_relay)
            if cycle + 1 < CYCLES:
                ring[cycle + 1, plane] = mixed
                send_own(cycle + 1, plane)
            else:
                for row in range(rows):
                    evolved_ref[0, plane, pl.ds(row, SUBLANES, stride=rows), :] = mixed[row]
            difference = own - jnp.where(left_partner, by_partner, by_relay)
            gap = gap + jnp.sum(difference * difference, axis=0)
        sums[0, cycle] = gap
        if cycle + 1 < CYCLES:
            forward(cycle + 1)

    def sum_copy(away):
        return pltpu.make_async_remote_copy(
            src_ref=sums.at[0],
            dst_ref=sums.at[away],
            send_sem=sum_send.at[away],
            recv_sem=sum_recv.at[away],
            device_id=(image, lax.rem(domain + away, domain_count)),
            device_id_type=MESH,
        )

    def distance_copy(away):
        return pltpu.make_async_remote_copy(
            src_ref=distances.at[0],
            dst_ref=distances.at[away],
            send_sem=distance_send.at[away],
            recv_sem=distance_recv.at[away],
            device_id=(image + away, domain),
            device_id_type=MESH,
        )

    for away in range(1, domain_count):
        sum_copy(away).start()
    for away in range(1, domain_count):
        sum_copy(away).wait_recv()
    total_cells = window * ny * nz
    for cycle in range(CYCLES):
        gap = sums[0, cycle]
        for away in range(1, domain_count):
            gap = gap + sums[away, cycle]
        gap = jnp.sum(jnp.sum(gap, axis=0, keepdims=True), axis=1, keepdims=True)
        distance = jnp.sqrt(gap / total_cells + epsilon)
        distance = jnp.where(jnp.full((1, 1), image, jnp.int32) == 0, 0.0, distance)
        distances[0, cycle : cycle + 1, :] = jnp.broadcast_to(distance, (1, nz))
    for away in range(1, image_count):
        @pl.when(image + away < image_count)
        def _():
            distance_copy(away).start()

    arclength_ref[...] = distances[0, :CYCLES, :1]
    for away in range(1, image_count):
        @pl.when(image >= away)
        def _():
            distance_copy(away).wait_recv()
            arclength_ref[...] = arclength_ref[...] + distances[away, :CYCLES, :1]

    for cycle in range(CYCLES):
        for plane in range(planes):
            partner_copy(cycle, plane).wait_send()

            @pl.when(has_onward)
            def _():
                relay_copy(cycle, plane).wait_send()

    for away in range(1, domain_count):
        sum_copy(away).wait_send()
    for away in range(1, image_count):
        @pl.when(image + away < image_count)
        def _():
            distance_copy(away).wait_send()


def per_device(field, mobility, lower, weights):
    domain_count = lax.axis_size("domain")
    image_count = lax.axis_size("image")
    planes, ny, nz = mobility.shape
    rows = ny // SUBLANES
    window = domain_count * planes
    messages = 2 * (domain_count // 2 - 1) + 1
    block = (planes, rows, SUBLANES, nz)
    whole = (window, rows, SUBLANES, nz)
    dma = pltpu.SemaphoreType.DMA
    anywhere = pl.BlockSpec(memory_space=pl.ANY)
    vmem = pl.BlockSpec(memory_space=pltpu.VMEM)
    smem = pl.BlockSpec(memory_space=pltpu.SMEM)
    evolved, arclength = pl.pallas_call(
        functools.partial(kernel, domain_count, image_count),
        out_shape=(
            jax.ShapeDtypeStruct(field.shape, jnp.float32),
            jax.ShapeDtypeStruct((CYCLES, 1), jnp.float32),
        ),
        in_specs=[anywhere, anywhere, smem, smem],
        out_specs=(vmem, vmem),
        scratch_shapes=[
            pltpu.VMEM((2, planes, ny, nz), jnp.float32),
            pltpu.VMEM((CYCLES + 1,) + whole, jnp.float32),
            pltpu.VMEM(whole, jnp.float32),
            pltpu.VMEM(whole, jnp.float32),
            pltpu.VMEM((CYCLES,) + block, jnp.float32),
            pltpu.VMEM((CYCLES,) + block, jnp.float32),
            pltpu.VMEM((domain_count, CYCLES, SUBLANES, nz), jnp.float32),
            pltpu.VMEM((image_count, SUBLANES, nz), jnp.float32),
            dma((2,)),
            dma((CYCLES + 1, messages, planes)),
            dma((CYCLES + 1, messages, planes)),
            dma((CYCLES, planes)),
            dma((CYCLES, planes)),
            dma((CYCLES, planes)),
            dma((CYCLES, planes)),
            dma((domain_count,)),
            dma((domain_count,)),
            dma((image_count,)),
            dma((image_count,)),
        ],
        compiler_params=pltpu.CompilerParams(collective_id=0, has_side_effects=True, vmem_limit_bytes=32 * 1024 * 1024),
    )(field, mobility, lower, weights)
    return evolved, arclength


def solution(mesh):
    return jax.shard_map(
        per_device,
        mesh=mesh,
        in_specs=(
            P("image", "domain", None, None),
            P("domain", None, None),
            P(None, "image"),
            P(None, "image"),
        ),
        out_specs=(P("image", "domain", None, None), P(None, "image")),
        check_vma=False,
    )
```

time: 146 us -> 63.3 us (0.43)
  the two profiles are of different devices: /device:TPU:0 before, /device:TPU:8 now
where the time goes in v1:
time: 63.3 us; the launch traced here: 63.1 us
  Pallas kernels  58.5 us (92%)
  local copies, waits for them, and re-layouts  3.9 us (6%)
  between operations  0.65 us (1%)
    pallas_call x1, Pallas kernels, per_device(): pl.pallas_call(functools.partial(kernel, domain_count, image_count), out_...  58.5 us
    unnamed x9, local copies, waits for them, and re-layouts  3.31 us

profile of v1, /device:TPU:8, one launch (start us, length us, event | category | flops | bytes accessed | tf_op | source)
XLA Modules:
  0.0 63.1 jit_solution(14543518168213687545)
XLA Ops:
  0.6 0.0 copy-start.2
  0.6 0.7 %copy.6.lower_ref = s32[2,1]{1,0:T(2,128)S(1)} copy(s32[2,1]{0,1:T(1,128)} %param.6) | data formatting | bytes 16 | tf_op args[2]
  1.4 0.0 copy-done.2
  1.4 0.1 copy.7.weights_ref
  1.5 0.0 copy-start
  1.5 0.9 %copy-done = f32[1,4,64,128]{3,2,1,0:T(8,128)S(1)} copy-done((f32[1,4,64,128]{3,2,1,0:T(8,128)S(1)}, f32[1,4,64,128]{3,2,1,0:T(8,128)}, u32[]{:S(2)}) %copy-start) | copy-done | bytes 131096
  2.4 0.0 copy-start.1
  2.4 0.9 %copy-done.1 = f32[4,64,128]{2,1,0:T(8,128)S(1)} copy-done((f32[4,64,128]{2,1,0:T(8,128)S(1)}, f32[4,64,128]{2,1,0:T(8,128)}, u32[]{:S(2)}) %copy-start.1) | copy-done | bytes 131096
  3.3 58.5 %shard_map.59 = (f32[1,4,64,128]{3,2,1,0:T(8,128)S(1)}, f32[2,1]{1,0:T(2,128)S(1)}) custom-call(f32[1,4,64,128]{3,2,1,0:T(8,128)S(1)} %copy-done, f32[4,64,128]{2,1,0:T(8,128)S(1)} %copy-done.1, s32[2,1]{1,0:T(2,128)S(1)} %copy.6.lower_ref, f32[2,1]{1,0:T(2,128)S(1)} %copy.7.weights_ref), custom_call_target="tpu_custom_call" | custom-call | tf_op jit(solution)/shard_map/pallas_call | solution.py:336
  61.8 0.6 copy.8
  62.4 0.7 %copy.10 = f32[1,4,64,128]{3,2,1,0:T(8,128)} copy(f32[1,4,64,128]{3,2,1,0:T(8,128)S(1)} %get-tuple-element.6) | data formatting | bytes 262144
Async XLA Ops:
  0.6 0.8 %copy-start.2 = (f32[2,1]{0,1:T(1,128)S(1)}, f32[2,1]{0,1:T(1,128)}, u32[]{:S(2)}) copy-start(f32[2,1]{0,1:T(1,128)} %param.7) | copy-start | bytes 28
  1.5 0.9 %copy-start = (f32[1,4,64,128]{3,2,1,0:T(8,128)S(1)}, f32[1,4,64,128]{3,2,1,0:T(8,128)}, u32[]{:S(2)}) copy-start(f32[1,4,64,128]{3,2,1,0:T(8,128)} %field_ref.1) | copy-start | bytes 393220
  2.4 0.9 %copy-start.1 = (f32[4,64,128]{2,1,0:T(8,128)S(1)}, f32[4,64,128]{2,1,0:T(8,128)}, u32[]{:S(2)}) copy-start(f32[4,64,128]{2,1,0:T(8,128)} %mobility_ref.1) | copy-start | bytes 393220

commit v2 on v1

--- a/solution.py
+++ b/solution.py
@@ -22,10 +22,12 @@
     image_count,
     field_ref,
     mobility_ref,
+    lower_hbm,
+    weights_hbm,
+    evolved_ref,
+    arclength_ref,
     lower_ref,
     weights_ref,
-    evolved_ref,
-    arclength_ref,
     stage,
     ring,
     potential,
@@ -57,6 +59,10 @@
     mobility_copy = pltpu.make_async_copy(mobility_ref, stage.at[1], stage_sem.at[1])
     field_copy.start()
     mobility_copy.start()
+    lower_copy = pltpu.make_async_copy(lower_hbm, lower_ref, stage_sem.at[2])
+    weights_copy = pltpu.make_async_copy(weights_hbm, weights_ref, stage_sem.at[3])
+    lower_copy.start()
+    weights_copy.start()
 
     barrier = pltpu.get_barrier_semaphore()
     for away in range(1, domain_count):
@@ -137,50 +143,52 @@
     def previous_column(value):
         return pltpu.roll(value, 1, 2)
 
+    def span(width, reach):
+        if width + 2 * reach >= window:
+            return list(range(window))
+        return [index % window for index in range(-reach, width + reach)]
+
+    def sweep(buffer, reach):
+        for index in span(planes, reach + 1):
+            here = ring[buffer, index]
+            around = ring[buffer, (index + 1) % window] + ring[buffer, (index - 1) % window]
+            around = around + (next_row(here) + previous_row(here))
+            around = around + (next_column(here) + previous_column(here))
+            square = here * here
+            potential[index] = here * (square + (6.0 * stiffness - 1.0)) - stiffness * around
+            below = 1.0 + square
+            inverse = pl.reciprocal(below, approx=True)
+            inverse = inverse * (2.0 - below * inverse)
+            motion[index] = ring[CYCLES, index] * inverse
+        order = span(planes, reach)
+
+        def flux_after(index):
+            after = (index + 1) % window
+            return (motion[index] + motion[after]) * (potential[after] - potential[index])
+
+        entering = flux_after((order[0] - 1) % window)
+        for index in order:
+            here, mobile = potential[index], motion[index]
+            leaving = flux_after(index)
+            along_row = (mobile + next_row(mobile)) * (next_row(here) - here)
+            along_column = (mobile + next_column(mobile)) * (next_column(here) - here)
+            change = (leaving - entering) + (along_row - previous_row(along_row))
+            change = change + (along_column - previous_column(along_column))
+            ring[buffer, index] = ring[buffer, index] + (0.5 * time_step) * change
+            entering = leaving
+
     def advance(buffer):
-        def step(number, carry):
-            reach = 2 * (STEPS - 1 - number)
-            offset = (2 * STEPS // window + 1) * window
-
-            def place(index):
-                return lax.rem(index, window)
-
-            def potentials(group, carry):
-                base = offset - reach - 1 + group * planes
-                layers = [ring[buffer, place(base - 1 + k)] for k in range(planes + 2)]
-                for k in range(planes):
-                    here = layers[k + 1]
-                    around = (layers[k] + layers[k + 2]) + (next_row(here) + previous_row(here))
-                    around = around + (next_column(here) + previous_column(here))
-                    square = here * here
-                    potential[place(base + k)] = here * (square + (6.0 * stiffness - 1.0)) - stiffness * around
-                    below = 1.0 + square
-                    inverse = pl.reciprocal(below, approx=True)
-                    inverse = inverse * (2.0 - below * inverse)
-                    motion[place(base + k)] = ring[CYCLES, place(base + k)] * inverse
-                return carry
-
-            def changes(group, carry):
-                base = offset - reach + group * planes
-                level = [potential[place(base - 1 + k)] for k in range(planes + 2)]
-                speed = [motion[place(base - 1 + k)] for k in range(planes + 2)]
-                flux = [(speed[k] + speed[k + 1]) * (level[k + 1] - level[k]) for k in range(planes + 1)]
-                for k in range(planes):
-                    here, mobile = level[k + 1], speed[k + 1]
-                    along_row = (mobile + next_row(mobile)) * (next_row(here) - here)
-                    along_column = (mobile + next_column(mobile)) * (next_column(here) - here)
-                    change = (flux[k + 1] - flux[k]) + (along_row - previous_row(along_row))
-                    change = change + (along_column - previous_column(along_column))
-                    ring[buffer, place(base + k)] = ring[buffer, place(base + k)] + (0.5 * time_step) * change
-                return carry
-
-            potential_groups = jnp.minimum(domain_count, (2 * planes + 2 * reach + 1) // planes)
-            change_groups = jnp.minimum(domain_count, (2 * planes + 2 * reach - 1) // planes)
-            lax.fori_loop(0, potential_groups, potentials, 0)
-            lax.fori_loop(0, change_groups, changes, 0)
+        reaches = [2 * (STEPS - 1 - number) for number in range(STEPS)]
+        full = [reach for reach in reaches if planes + 2 * reach >= window]
+
+        def full_sweep(number, carry):
+            sweep(buffer, full[0])
             return carry
 
-        lax.fori_loop(0, STEPS, step, 0)
+        if full:
+            lax.fori_loop(0, len(full), full_sweep, 0)
+        for reach in reaches[len(full) :]:
+            sweep(buffer, reach)
 
     image_parity = lax.rem(image, 2)
     odd = image_parity == 1
@@ -214,6 +222,8 @@
     def _():
         relay_field[...] = jnp.zeros(relay_field.shape, jnp.float32)
 
+    lower_copy.wait()
+    weights_copy.wait()
     for cycle in range(CYCLES):
         finish_gather(cycle)
         if cycle == 0:
@@ -332,16 +342,17 @@
     dma = pltpu.SemaphoreType.DMA
     anywhere = pl.BlockSpec(memory_space=pl.ANY)
     vmem = pl.BlockSpec(memory_space=pltpu.VMEM)
-    smem = pl.BlockSpec(memory_space=pltpu.SMEM)
     evolved, arclength = pl.pallas_call(
         functools.partial(kernel, domain_count, image_count),
         out_shape=(
             jax.ShapeDtypeStruct(field.shape, jnp.float32),
             jax.ShapeDtypeStruct((CYCLES, 1), jnp.float32),
         ),
-        in_specs=[anywhere, anywhere, smem, smem],
+        in_specs=[anywhere] * 4,
         out_specs=(vmem, vmem),
         scratch_shapes=[
+            pltpu.SMEM(lower.shape, jnp.int32),
+            pltpu.SMEM(weights.shape, jnp.float32),
             pltpu.VMEM((2, planes, ny, nz), jnp.float32),
             pltpu.VMEM((CYCLES + 1,) + whole, jnp.float32),
             pltpu.VMEM(whole, jnp.float32),
@@ -350,7 +361,7 @@
             pltpu.VMEM((CYCLES,) + block, jnp.float32),
             pltpu.VMEM((domain_count, CYCLES, SUBLANES, nz), jnp.float32),
             pltpu.VMEM((image_count, SUBLANES, nz), jnp.float32),
-            dma((2,)),
+            dma((4,)),
             dma((CYCLES + 1, messages, planes)),
             dma((CYCLES + 1, messages, planes)),
             dma((CYCLES, planes)),

time: 63.3 us -> 64.4 us (1.017)
  Pallas kernels: 58.5 us -> 59.7 us
    pallas_call x1, Pallas kernels: 58.5 us -> 59.7 us  [per_device(): pl.pallas_call(functools.partial(kernel, domain_count, image_count), out_...]
where the time goes in v2:
time: 64.4 us; the launch traced here: 64.3 us
  Pallas kernels  59.7 us (93%)
  local copies, waits for them, and re-layouts  3.9 us (6%)
  between operations  0.65 us (1%)
    pallas_call x1, Pallas kernels, per_device(): pl.pallas_call(functools.partial(kernel, domain_count, image_count), out_...  59.7 us
    unnamed x9, local copies, waits for them, and re-layouts  3.31 us

profile of v2, /device:TPU:8, one launch (start us, length us, event | category | flops | bytes accessed | tf_op | source)
XLA Modules:
  0.0 64.3 jit_solution(11923586225670532630)
XLA Ops:
  0.6 0.0 copy-start.2
  0.6 0.7 %copy.6.lower_hbm = s32[2,1]{1,0:T(2,128)S(1)} copy(s32[2,1]{0,1:T(1,128)} %param.6) | data formatting | bytes 16 | tf_op args[2]
  1.4 0.0 copy-done.2
  1.4 0.1 copy.7.weights_hbm
  1.5 0.0 copy-start
  1.5 0.9 %copy-done = f32[1,4,64,128]{3,2,1,0:T(8,128)S(1)} copy-done((f32[1,4,64,128]{3,2,1,0:T(8,128)S(1)}, f32[1,4,64,128]{3,2,1,0:T(8,128)}, u32[]{:S(2)}) %copy-start) | copy-done | bytes 131096
  2.4 0.0 copy-start.1
  2.4 0.9 %copy-done.1 = f32[4,64,128]{2,1,0:T(8,128)S(1)} copy-done((f32[4,64,128]{2,1,0:T(8,128)S(1)}, f32[4,64,128]{2,1,0:T(8,128)}, u32[]{:S(2)}) %copy-start.1) | copy-done | bytes 131096
  3.3 59.7 %shard_map.59 = (f32[1,4,64,128]{3,2,1,0:T(8,128)S(1)}, f32[2,1]{1,0:T(2,128)S(1)}) custom-call(f32[1,4,64,128]{3,2,1,0:T(8,128)S(1)} %copy-done, f32[4,64,128]{2,1,0:T(8,128)S(1)} %copy-done.1, s32[2,1]{1,0:T(2,128)S(1)} %copy.6.lower_hbm, f32[2,1]{1,0:T(2,128)S(1)} %copy.7.weights_hbm), custom_call_target="tpu_custom_call" | custom-call | tf_op jit(solution)/shard_map/pallas_call | solution.py:345
  63.0 0.6 copy.8
  63.6 0.7 %copy.10 = f32[1,4,64,128]{3,2,1,0:T(8,128)} copy(f32[1,4,64,128]{3,2,1,0:T(8,128)S(1)} %get-tuple-element.6) | data formatting | bytes 262144
Async XLA Ops:
  0.6 0.8 %copy-start.2 = (f32[2,1]{0,1:T(1,128)S(1)}, f32[2,1]{0,1:T(1,128)}, u32[]{:S(2)}) copy-start(f32[2,1]{0,1:T(1,128)} %param.7) | copy-start | bytes 28
  1.5 0.9 %copy-start = (f32[1,4,64,128]{3,2,1,0:T(8,128)S(1)}, f32[1,4,64,128]{3,2,1,0:T(8,128)}, u32[]{:S(2)}) copy-start(f32[1,4,64,128]{3,2,1,0:T(8,128)} %field_ref.1) | copy-start | bytes 393220
  2.4 0.9 %copy-start.1 = (f32[4,64,128]{2,1,0:T(8,128)S(1)}, f32[4,64,128]{2,1,0:T(8,128)}, u32[]{:S(2)}) copy-start(f32[4,64,128]{2,1,0:T(8,128)} %mobility_ref.1) | copy-start | bytes 393220

commit v3 on v2

--- a/solution.py
+++ b/solution.py
@@ -149,33 +149,59 @@
         return [index % window for index in range(-reach, width + reach)]
 
     def sweep(buffer, reach):
-        for index in span(planes, reach + 1):
+        def turned(index):
             here = ring[buffer, index]
+            return here, next_column(here), previous_column(here)
+
+        def settle(index, here, after, before):
             around = ring[buffer, (index + 1) % window] + ring[buffer, (index - 1) % window]
             around = around + (next_row(here) + previous_row(here))
-            around = around + (next_column(here) + previous_column(here))
+            around = around + (after + before)
             square = here * here
             potential[index] = here * (square + (6.0 * stiffness - 1.0)) - stiffness * around
             below = 1.0 + square
             inverse = pl.reciprocal(below, approx=True)
             inverse = inverse * (2.0 - below * inverse)
             motion[index] = ring[CYCLES, index] * inverse
+
+        order = span(planes, reach + 1)
+        ready = turned(order[0])
+        for number, index in enumerate(order):
+            later = turned(order[number + 1]) if number + 1 < len(order) else None
+            settle(index, *ready)
+            ready = later
+
         order = span(planes, reach)
 
         def flux_after(index):
             after = (index + 1) % window
             return (motion[index] + motion[after]) * (potential[after] - potential[index])
 
-        entering = flux_after((order[0] - 1) % window)
-        for index in order:
+        def shifted(index):
+            return next_column(potential[index]), next_column(motion[index])
+
+        def column_flux(index, level, speed):
+            along = (motion[index] + speed) * (level - potential[index])
+            return along, previous_column(along)
+
+        def finish(index, entering, along, along_before):
             here, mobile = potential[index], motion[index]
             leaving = flux_after(index)
             along_row = (mobile + next_row(mobile)) * (next_row(here) - here)
-            along_column = (mobile + next_column(mobile)) * (next_column(here) - here)
             change = (leaving - entering) + (along_row - previous_row(along_row))
-            change = change + (along_column - previous_column(along_column))
+            change = change + (along - along_before)
             ring[buffer, index] = ring[buffer, index] + (0.5 * time_step) * change
-            entering = leaving
+            return leaving
+
+        entering = flux_after((order[0] - 1) % window)
+        moved, along = {}, {}
+        for tick in range(len(order) + 2):
+            if tick < len(order):
+                moved[tick] = shifted(order[tick])
+            if 1 <= tick <= len(order):
+                along[tick - 1] = column_flux(order[tick - 1], *moved.pop(tick - 1))
+            if tick >= 2:
+                entering = finish(order[tick - 2], entering, *along.pop(tick - 2))
 
     def advance(buffer):
         reaches = [2 * (STEPS - 1 - number) for number in range(STEPS)]
@@ -233,13 +259,13 @@
         advance(cycle)
         for plane in range(planes):
             partner_copy(cycle, plane).start()
-        weight = weights_ref[cycle, 0]
-        from_left = lower_ref[cycle, 0] < image
+        shape = (rows, SUBLANES, nz)
+        weight = weights_ref[0, cycle]
+        from_left = lower_ref[0, cycle] < image
         own_share = jnp.where(from_left, 1.0 - weight, weight)
         other_share = jnp.where(from_left, weight, 1.0 - weight)
-        from_left = jnp.where(from_left, 1, 0)
-        use_partner = jnp.full((rows, SUBLANES, nz), from_left, jnp.int32) == image_parity
-        left_partner = jnp.full((rows, SUBLANES, nz), image_parity, jnp.int32) == 1
+        use_partner = jnp.full(shape, jnp.where(from_left, 1, 0), jnp.int32) == image_parity
+        left_partner = jnp.full(shape, image_parity, jnp.int32) == 1
         for plane in range(planes):
             partner_copy(cycle, plane).wait_recv()
 
@@ -294,6 +320,8 @@
     for away in range(1, domain_count):
         sum_copy(away).wait_recv()
     total_cells = window * ny * nz
+    lane = lax.broadcasted_iota(jnp.int32, (1, nz), 1)
+    by_cycle = jnp.zeros((1, nz), jnp.float32)
     for cycle in range(CYCLES):
         gap = sums[0, cycle]
         for away in range(1, domain_count):
@@ -301,18 +329,19 @@
         gap = jnp.sum(jnp.sum(gap, axis=0, keepdims=True), axis=1, keepdims=True)
         distance = jnp.sqrt(gap / total_cells + epsilon)
         distance = jnp.where(jnp.full((1, 1), image, jnp.int32) == 0, 0.0, distance)
-        distances[0, cycle : cycle + 1, :] = jnp.broadcast_to(distance, (1, nz))
+        by_cycle = jnp.where(lane == cycle, distance, by_cycle)
+    distances[0, :1, :] = by_cycle
     for away in range(1, image_count):
         @pl.when(image + away < image_count)
         def _():
             distance_copy(away).start()
 
-    arclength_ref[...] = distances[0, :CYCLES, :1]
+    arclength_ref[...] = distances[0, :1, :CYCLES]
     for away in range(1, image_count):
         @pl.when(image >= away)
         def _():
             distance_copy(away).wait_recv()
-            arclength_ref[...] = arclength_ref[...] + distances[away, :CYCLES, :1]
+            arclength_ref[...] = arclength_ref[...] + distances[away, :1, :CYCLES]
 
     for cycle in range(CYCLES):
         for plane in range(planes):
@@ -340,19 +369,19 @@
     block = (planes, rows, SUBLANES, nz)
     whole = (window, rows, SUBLANES, nz)
     dma = pltpu.SemaphoreType.DMA
-    anywhere = pl.BlockSpec(memory_space=pl.ANY)
+    hbm = pl.BlockSpec(memory_space=pltpu.HBM)
     vmem = pl.BlockSpec(memory_space=pltpu.VMEM)
     evolved, arclength = pl.pallas_call(
         functools.partial(kernel, domain_count, image_count),
         out_shape=(
             jax.ShapeDtypeStruct(field.shape, jnp.float32),
-            jax.ShapeDtypeStruct((CYCLES, 1), jnp.float32),
+            jax.ShapeDtypeStruct((1, CYCLES), jnp.float32),
         ),
-        in_specs=[anywhere] * 4,
+        in_specs=[hbm] * 4,
         out_specs=(vmem, vmem),
         scratch_shapes=[
-            pltpu.SMEM(lower.shape, jnp.int32),
-            pltpu.SMEM(weights.shape, jnp.float32),
+            pltpu.SMEM((1, CYCLES), jnp.int32),
+            pltpu.SMEM((1, CYCLES), jnp.float32),
             pltpu.VMEM((2, planes, ny, nz), jnp.float32),
             pltpu.VMEM((CYCLES + 1,) + whole, jnp.float32),
             pltpu.VMEM(whole, jnp.float32),
@@ -373,9 +402,9 @@
             dma((image_count,)),
             dma((image_count,)),
         ],
-        compiler_params=pltpu.CompilerParams(collective_id=0, has_side_effects=True, vmem_limit_bytes=32 * 1024 * 1024),
-    )(field, mobility, lower, weights)
-    return evolved, arclength
+        compiler_params=pltpu.CompilerParams(collective_id=0, has_side_effects=True, vmem_limit_bytes=63 * 1024 * 1024),
+    )(field, mobility, lower.T, weights.T)
+    return evolved, arclength.T
 
 
 def solution(mesh):

time: 64.4 us -> 55.5 us (0.86)
  Pallas kernels: 59.7 us -> 52.6 us
  local copies, waits for them, and re-layouts: 3.9 us -> 2.08 us
    pallas_call x1, Pallas kernels: 59.7 us -> 52.6 us  [per_device(): pl.pallas_call(functools.partial(kernel, domain_count, image_count), out_...]
    unnamed x9 -> x4, local copies, waits for them, and re-layouts: 3.31 us -> 2.08 us
where the time goes in v3:
time: 55.5 us; the launch traced here: 55.4 us
  Pallas kernels  52.6 us (95%)
  local copies, waits for them, and re-layouts  2.08 us (4%)
  between operations  0.65 us (1%)
    pallas_call x1, Pallas kernels, per_device(): pl.pallas_call(functools.partial(kernel, domain_count, image_count), out_...  52.6 us
    unnamed x4, local copies, waits for them, and re-layouts  2.08 us

profile of v3, /device:TPU:8, one launch (start us, length us, event | category | flops | bytes accessed | tf_op | source)
XLA Modules:
  0.0 55.4 jit_solution(3108185158196712365)
XLA Ops:
  0.6 52.6 %shard_map.59 = (f32[1,4,64,128]{3,2,1,0:T(8,128)}, f32[1,2]{1,0:T(1,128)}) custom-call(f32[1,4,64,128]{3,2,1,0:T(8,128)} %field_ref.1, f32[4,64,128]{2,1,0:T(8,128)} %mobility_ref.1, s32[1,2]{1,0:T(1,128)} %bitcast.3, f32[1,2]{1,0:T(1,128)} %bitcast.4), custom_call_target="tpu_custom_call" | custom-call | tf_op jit(solution)/shard_map/pallas_call | solution.py:374
  53.3 0.0 copy-start
  53.3 1.6 %copy.8 = f32[1,4,64,128]{3,2,1,0:T(8,128)} copy(f32[1,4,64,128]{3,2,1,0:T(8,128)} %get-tuple-element.8) | data formatting | bytes 262144
  54.9 0.0 copy-done
  54.9 0.5 copy.9
Async XLA Ops:
  53.3 1.6 %copy-start = (f32[1,2]{1,0:T(1,128)S(1)}, f32[1,2]{1,0:T(1,128)}, u32[]{:S(2)}) copy-start(f32[1,2]{1,0:T(1,128)} %get-tuple-element.5) | copy-start | bytes 28
